TPU v7x, 128 devices: a whole 4x4x4 slice. The times are simulated.
128 devices in a mesh: grp: 8 (over x, core), dp: 16 (over z, y).
Axes of the slice: x: 4, y: 4, z: 4, core: 2. Of those that a mesh axis runs over, the one named last changes fastest.
Arguments:
- visual: bfloat16 [16, 1024, 3200], P('dp', 'grp'), may hold values from -6 to 6
- projector: bfloat16 [3200, 8192], P('dp', 'grp'), may hold values from -0.109375 to 0.109375
- key_weight: bfloat16 [8192, 512], replicated, may hold values from -0.0625 to 0.0625
- norm_gain: bfloat16 [8192], replicated, may hold values from 0.099609375 to 1.8984375
- cotangent: bfloat16 [16, 4096, 512], P('dp', 'grp'), may hold values from -0.25 to 0.25
- residual: bfloat16 [51200, 8192], P('dp', 'grp'), may hold values from -0.796875 to 0.796875
- counts: int32 [16, 8, 8], P('dp'), may hold values from 0 to 4, as said below
- offsets: int32 [16, 8, 8], P('dp'), may hold values from 0 to 512, as said below
Outputs:
- weight_grad: float32 [3200, 8192], P('dp', 'grp')
- residual_out: bfloat16 [51200, 8192], P('dp', 'grp')
Inputs may be any that keep to these rules, and one draw needn't show every extreme that they name: counts[d, s, b] tiles of 32 rows go from encoder shard s to backbone shard b; each source sends all 4 of its tiles, in order of destination; in every data index one backbone shard receives exactly 8 tiles and none receives more, and some source sends all its tiles to one backbone shard. The counts[d, s, b] * 32 rows that backbone shard b receives from source s start at offsets[d, s, b] of its 512 positions; nonempty blocks lie in order of source, do not intersect and end at or before 512; where counts[d, s, b] is 0, offsets[d, s, b] is 512.
All inputs are finite; a program needn't handle non-finite values.
Results may differ from a plain program's by a relative error of at most 0.015.
Values may be sent and summed in bfloat16 or wider, within the bound.
A program may use at most 128 MiB of HBM per device.

v0:
```python
import jax
import jax.numpy as jnp
from jax import lax
from jax.sharding import PartitionSpec as P

TROWS = 32
IN_CAP = 8


norm_eps = 1e-06
clip_limit = 0.5


def tile_tables(route_table, start_table, tile_count):
    groups = route_table.shape[0]
    dest_ids = jnp.arange(groups, dtype=jnp.int32)
    tile_ids = jnp.arange(tile_count, dtype=jnp.int32)
    through = jnp.cumsum(route_table, axis=1, dtype=jnp.int32)
    before_dest = through - route_table
    before_source = jnp.cumsum(route_table, axis=0, dtype=jnp.int32) - route_table
    target = jnp.sum(
        (through[:, None, :] <= tile_ids[None, :, None]).astype(jnp.int32), axis=2, dtype=jnp.int32
    )
    chosen = (target[:, :, None] == dest_ids[None, None, :]).astype(jnp.int32)
    within = tile_ids[None, :] - jnp.sum(chosen * before_dest[:, None, :], axis=2, dtype=jnp.int32)
    slot_tile = jnp.sum(chosen * before_source[:, None, :], axis=2, dtype=jnp.int32) + within
    position = jnp.sum(chosen * start_table[:, None, :], axis=2, dtype=jnp.int32) + within * TROWS
    return (target, slot_tile, position)


def backbone_grad(rows, key_rows, key_weight, norm_gain):
    values = rows.astype(jnp.float32)
    inverse = lax.rsqrt(jnp.mean(values * values, axis=-1, keepdims=True) + norm_eps)
    normed = values * inverse
    upstream = lax.dot_general(
        key_rows, key_weight, (((1,), (1,)), ((), ())), preferred_element_type=jnp.float32
    )
    scaled = norm_gain.astype(jnp.float32) * upstream
    inner_mean = jnp.mean(normed * scaled, axis=-1, keepdims=True)
    return (inverse * (scaled - normed * inner_mean)).astype(jnp.bfloat16)


def per_device(visual, projector, key_weight, norm_gain, cotangent, residual, counts, offsets):
    groups = lax.axis_size("grp")
    own_index = lax.axis_index("grp")
    rows_dev = visual.shape[1]
    tile_count = rows_dev // TROWS
    block_width = projector.shape[1]
    row_offsets = jnp.arange(TROWS, dtype=jnp.int32)
    target, slot_tile, position = tile_tables(counts[0], offsets[0], tile_count)
    gathered = lax.all_gather(visual[0], "grp", axis=0, tiled=True)
    projected = jnp.dot(
        gathered,
        lax.all_gather(projector, "dp", axis=0, tiled=True),
        preferred_element_type=jnp.float32,
    ).astype(jnp.bfloat16)
    key_table = cotangent[0]
    capacity = IN_CAP
    length = capacity * TROWS
    sources = jnp.arange(groups, dtype=jnp.int32)
    flat_tile = sources[:, None] * tile_count + jnp.arange(tile_count, dtype=jnp.int32)[None, :]
    matched = (target[None, None] == sources[:, None, None, None]) & (
        slot_tile[None, None] == jnp.arange(capacity, dtype=jnp.int32)[None, :, None, None]
    )
    hit_table = matched.astype(jnp.int32)
    filled = jnp.sum(hit_table, axis=(2, 3), dtype=jnp.int32) > 0
    source_tile = jnp.sum(hit_table * flat_tile, axis=(2, 3), dtype=jnp.int32)
    tile_place = jnp.sum(hit_table * position, axis=(2, 3), dtype=jnp.int32)
    row_filled = jnp.broadcast_to(filled[:, :, None], (groups, capacity, TROWS)).reshape(
        groups, length
    )
    row_index = (source_tile[:, :, None] * TROWS + row_offsets).reshape(-1)
    outgoing = jnp.take(projected, row_index, axis=0).reshape(groups, length, block_width)
    outgoing = jnp.where(row_filled[:, :, None], outgoing, jnp.zeros_like(outgoing))
    arrived = lax.all_to_all(outgoing, "grp", split_axis=0, concat_axis=2, tiled=True)
    mine_place = tile_place[own_index]
    mine_filled = row_filled[own_index]
    lookup = (mine_place[:, None] + row_offsets).reshape(-1)
    key_rows = jnp.take(key_table, lookup, axis=0)
    key_rows = jnp.where(mine_filled[:, None], key_rows, jnp.zeros_like(key_rows))
    row_grads = backbone_grad(arrived[0], key_rows, key_weight, norm_gain)
    returned = lax.all_to_all(row_grads[None], "grp", split_axis=2, concat_axis=0, tiled=True)
    flat_index = ((target * capacity + slot_tile)[:, :, None] * TROWS + row_offsets).reshape(-1)
    row_grad = jnp.take(returned.reshape(groups * length, block_width), flat_index, axis=0)
    grad_term = lax.dot_general(
        gathered, row_grad, (((0,), (0,)), ((), ())), preferred_element_type=jnp.float32
    )
    carried = grad_term + residual.astype(jnp.float32)
    clipped = jnp.clip(carried, -clip_limit, clip_limit)
    quantized = clipped.astype(jnp.bfloat16)
    residual_out = (carried - clipped).astype(jnp.bfloat16)
    weight_grad = lax.psum_scatter(
        quantized.astype(jnp.float32).astype(jnp.bfloat16), "dp", scatter_dimension=0, tiled=True
    ).astype(jnp.float32)
    return (weight_grad, residual_out)


def solution(mesh):
    placed = (
        P("dp", "grp", None),
        P("dp", "grp"),
        P(),
        P(),
        P("dp", "grp", None),
        P("dp", "grp"),
        P("dp", None, None),
        P("dp", None, None),
    )
    return jax.shard_map(
        per_device,
        mesh=mesh,
        in_specs=placed,
        out_specs=(P("dp", "grp"), P("dp", "grp")),
        check_vma=False,
    )
```

profile of v0, /device:TPU:0, one launch (start us, length us, event | category | flops | bytes accessed | tf_op | source)
XLA Modules:
  0.0 521.5 jit_solution(14231353054238653853)
XLA Ops:
  13.1 41.1 %all-gather.6.cloned.1.call-done = bf16[1,1024,3200]{2,1,0:T(8,128)(2,1)} async-done(((bf16[1,128,3200]{2,1,0:T(8,128)(2,1)}), bf16[1,1024,3200]{2,1,0:T(8,128)(2,1)}) %all-gather.6.cloned.1.call-update) | async-done | bytes 6553616 | tf_op jit(solution)/shard_map/all_gather | solution.py:51
  54.2 64.8 %all-gather.4.cloned.1.call-done = bf16[3200,1024]{1,0:T(8,128)(2,1)} async-done(((bf16[200,1024]{1,0:T(8,128)(2,1)}), bf16[3200,1024]{1,0:T(8,128)(2,1)}) %all-gather.4.cloned.1.call-update) | async-done | bytes 6553616 | tf_op jit(solution)/shard_map/all_gather | solution.py:54
  119.0 11.2 %fusion.9 = bf16[1024,1024]{1,0:T(8,128)(2,1)S(1)} fusion(bf16[3200,1024]{1,0:T(8,128)(2,1)} %all-gather.4.cloned.1.call-done, bf16[1,1024,3200]{2,1,0:T(8,128)(2,1)} %all-gather.6.cloned.1.call-done), kind=kOutput, calls=%fused_computation.21 | convolution fusion | flops 6711934976 | bytes 15204352 | tf_op jit(solution)/shard_map/dot_general | solution.py:52
  130.2 9.6 %gather_fusion = bf16[2048,1024]{1,0:T(8,128)(2,1)} fusion(bf16[1024,1024]{1,0:T(8,128)(2,1)S(1)} %fusion.9, s32[2048]{0:T(1024)S(1)} %broadcast_clamp_fusion), kind=kCustom, calls=%fused_computation | custom fusion | bytes 8396800 | tf_op jit(solution)/shard_map/jit(_take)/gather | solution.py:73
  139.9 4.0 select_select_fusion
  143.8 4.7 all-to-all-start
  150.1 48.0 %all-to-all-done = bf16[8,256,1024]{2,1,0:T(8,128)(2,1)} async-done(((bf16[8,256,1024]{2,1,0:T(8,128)(2,1)}), bf16[8,256,1024]{2,1,0:T(8,128)(2,1)}, u32[]{:S(2)}, u32[]{:S(2)}) %all-to-all-start) | async-done | bytes 4194336 | tf_op jit(solution)/shard_map/all_to_all | solution.py:75
  198.1 3.2 fusion.27
  202.1 3.1 fusion.1
  205.3 11.2 %multiply_reduce_fusion = (f32[256]{0:T(256)S(1)}, f32[256,8192]{1,0:T(8,128)}) fusion(f32[256,8192]{1,0:T(8,128)S(1)} %bitcast.52, f32[256]{0:T(256)S(1)} %add_rsqrt_fusion, bf16[8192,512]{1,0:T(8,128)(2,1)} %param.10, bf16[256,512]{1,0:T(8,128)(2,1)S(1)} %gather_fusion.1, pred[256]{0:T(512)(128)(4,1)S(1)} %compare_and_fusion.2, ...), kind=kOutput, calls=%fused_computation.12 | convolution fusion | flops 2156134144 | bytes 25463296 | tf_op jit(solution)/shard_map/dot_general | solution.py:35
  216.5 5.7 %fusion.6 = bf16[1,256,8192]{2,1,0:T(8,128)(2,1)} fusion(f32[256,8192]{1,0:T(8,128)} %get-tuple-element.26, f32[256,8192]{1,0:T(8,128)S(1)} %bitcast.53, f32[256]{0:T(256)S(1)} %broadcast_multiply_fusion.1, f32[256]{0:T(256)S(1)} %add_rsqrt_fusion), kind=kLoop, calls=%fused_computation.17 | loop fusion | flops 10485760 | bytes 20973568 | tf_op jit(solution)/shard_map/broadcast_in_dim | solution.py:82
  222.2 17.9 %copy.36 = bf16[1,256,8192]{1,0,2:T(2,128)(2,1)} copy(bf16[1,256,8192]{2,1,0:T(8,128)(2,1)} %fusion.6) | data formatting | bytes 8388608 | tf_op jit(solution)/shard_map/broadcast_in_dim | solution.py:82
  240.6 43.5 %reduce.5 = bf16[8192,256]{1,0:T(8,128)(2,1)} reduce(bf16[8192,1,256]{2,1,0:T(2,128)(2,1)} %bitcast.54, bf16[]{:T(256)} %broadcast.209), dimensions={1}, to_apply=%bitcast.41.reduce_sub_computation | reduce | bytes 8388610
  284.1 7.0 %reshape.297 = bf16[8,2,131072]{2,1,0:T(2,128)(2,1)} reshape(bf16[8192,256]{1,0:T(8,128)(2,1)} %reduce.5) | data formatting | bytes 8388608
  291.1 4.5 all-to-all-start.1
  296.3 9.5 %copy.38 = bf16[3200,1024]{0,1:T(8,128)(2,1)} copy(bf16[3200,1024]{1,0:T(8,128)(2,1)} %param.13) | data formatting | bytes 13107200 | tf_op args[5]
  305.9 39.5 %all-to-all-done.1 = bf16[8,2,131072]{2,1,0:T(2,128)(2,1)} async-done(((bf16[8,2,131072]{2,1,0:T(2,128)(2,1)}), bf16[8,2,131072]{2,1,0:T(2,128)(2,1)}, u32[]{:S(2)}, u32[]{:S(2)}) %all-to-all-start.1) | async-done | bytes 4194336 | tf_op jit(solution)/shard_map/all_to_all | solution.py:82
  345.4 8.8 %reshape.298 = bf16[8192,1,256]{2,1,0:T(2,128)(2,1)} reshape(bf16[8,2,131072]{2,1,0:T(2,128)(2,1)} %all-to-all-done.1) | data formatting | bytes 8388608
  354.1 6.1 %copy.43 = bf16[1,256,8192]{1,2,0:T(8,128)(2,1)} copy(bf16[1,256,8192]{1,0,2:T(2,128)(2,1)} %bitcast.55) | data formatting | bytes 8388608
  360.2 6.5 %copy.37 = bf16[8,1,256,1024]{3,2,0,1:T(8,128)(2,1)} copy(bf16[8,1,256,1024]{2,3,0,1:T(8,128)(2,1)} %bitcast.56) | data formatting | bytes 8388608 | tf_op jit(solution)/shard_map/all_to_all | solution.py:82
  366.7 7.7 %gather_fusion.2 = bf16[1024,1024]{1,0:T(8,128)(2,1)S(1)} fusion(bf16[2048,1024]{1,0:T(8,128)(2,1)} %bitcast.51, s32[1024]{0:T(1024)S(1)} %broadcast_clamp_fusion.1), kind=kCustom, calls=%fused_computation.2 | custom fusion | bytes 4198400 | tf_op jit(solution)/shard_map/jit(_take)/gather | solution.py:84
  374.4 15.4 %fusion = (bf16[3200,1024]{0,1:T(8,128)(2,1)}, bf16[3200,1024]{0,1:T(8,128)(2,1)}) fusion(bf16[3200,1024]{0,1:T(8,128)(2,1)} %copy.38, bf16[1,1024,3200]{2,1,0:T(8,128)(2,1)} %all-gather.6.cloned.1.call-done, bf16[1024,1024]{1,0:T(8,128)(2,1)S(1)} %gather_fusion.2, pred[1024]{0:T(1024)(128)(4,1)S(1)} %compare_and_fusion.1), kind=kOutput, calls=%fused_computation.5 | convolution fusion | flops 6731595776 | bytes 28312576 | tf_op jit(solution)/shard_map/dot_general | solution.py:85
  391.6 9.6 %copy.40 = bf16[3200,1024]{1,0:T(8,128)(2,1)} copy(bf16[3200,1024]{0,1:T(8,128)(2,1)} %get-tuple-element.20) | data formatting | bytes 13107200
  401.2 111.2 %all-reduce.3.cloned.1.call-done = bf16[3200,1024]{0,1:T(8,128)(2,1)} async-done(((bf16[3200,1024]{0,1:T(8,128)(2,1)}), bf16[3200,1024]{0,1:T(8,128)(2,1)}) %all-reduce.3.cloned.1.call-update) | async-done | bytes 6553616
  (58 shorter events, 13.1 us)
Async XLA Ops:
  7.2 141.7 %copy-start = (bf16[1,512,512]{2,1,0:T(8,128)(2,1)S(1)}, bf16[1,512,512]{2,1,0:T(8,128)(2,1)}, u32[]{:S(2)}) copy-start(bf16[1,512,512]{2,1,0:T(8,128)(2,1)} %param.12) | copy-start | bytes 1572868
  7.2 47.0 %all-gather.6.cloned.1.call-start = ((), (), s32[]{:S(2)}) async-start(), calls=%async_computation.3 | async-start | bytes 7372800 | tf_op jit(solution)/shard_map/all_gather | solution.py:51
  7.9 111.1 %all-gather.4.cloned.1.call-start = ((), (), s32[]{:S(2)}) async-start(), calls=%async_computation.2 | async-start | bytes 6963200 | tf_op jit(solution)/shard_map/all_gather | solution.py:54
  139.9 9.0 %copy-start.2 = (bf16[8192]{0:T(1024)(128)(2,1)S(1)}, bf16[8192]{0:T(1024)(128)(2,1)}, u32[]{:S(2)}) copy-start(bf16[8192]{0:T(1024)(128)(2,1)} %param.11) | copy-start | bytes 49156
  143.8 54.2 %all-to-all-start = ((bf16[8,256,1024]{2,1,0:T(8,128)(2,1)}), bf16[8,256,1024]{2,1,0:T(8,128)(2,1)}, u32[]{:S(2)}, u32[]{:S(2)}) async-start(bf16[8,256,1024]{2,1,0:T(8,128)(2,1)} %select_select_fusion), calls=%async_computation | async-start | bytes 8388608 | tf_op jit(solution)/shard_map/all_to_all | solution.py:75
  291.1 54.2 %all-to-all-start.1 = ((bf16[8,2,131072]{2,1,0:T(2,128)(2,1)}), bf16[8,2,131072]{2,1,0:T(2,128)(2,1)}, u32[]{:S(2)}, u32[]{:S(2)}) async-start(bf16[8,2,131072]{2,1,0:T(2,128)(2,1)} %reshape.297), calls=%async_computation.1 | async-start | bytes 8388608 | tf_op jit(solution)/shard_map/all_to_all | solution.py:82
  295.7 216.7 %all-reduce.3.cloned.1.call-start = ((), (), s32[]{:S(2)}) async-start(), calls=%async_computation.4 | async-start | bytes 13107200
  389.7 0.7 copy-start.3
  391.6 123.4 %copy-start.1 = (bf16[1,512,512]{2,1,0:T(8,128)(2,1)S(1)}, bf16[1,512,512]{2,1,0:T(8,128)(2,1)}, u32[]{:S(2)}) copy-start(bf16[1,512,512]{2,1,0:T(8,128)(2,1)} %param.12) | copy-start | bytes 1572868
Sparse Core Ops, SparseCore 0:
  9.7 44.4 all-gather.5
  56.3 62.6 all-gather.3
  389.9 122.4 all-reduce.2
where the time goes:
time: 524 us; the launch traced here: 522 us
  waiting for transfers between devices  306 us (58%)
  local copies, waits for them, and re-layouts  88.3 us (17%)
  other arithmetic  65.2 us (12%)
  matrix products  37.8 us (7%)
  between operations  14.6 us (3%)
  starting transfers between devices  9.63 us (2%)
    unnamed x4, waiting for transfers between devices  113 us
    all_gather x1, waiting for transfers between devices, per_device(): lax.all_gather(projector, 'dp', axis=0, tiled=True)  64.8 us
    all_to_all x1, waiting for transfers between devices, per_device(): lax.all_to_all(outgoing, 'grp', split_axis=0, concat_axis=2, tiled=True)  48 us
    unnamed x2, other arithmetic  46.8 us
    unnamed x17, local copies, waits for them, and re-layouts  44.8 us
    all_gather x1, waiting for transfers between devices, per_device(): gathered = lax.all_gather(visual[0], 'grp', axis=0, tiled=True)  41.1 us
    all_to_all x1, waiting for transfers between devices, per_device(): lax.all_to_all(row_grads[None], 'grp', split_axis=2, concat_axis=0, tiled...  39.5 us
    broadcast_in_dim x1, local copies, waits for them, and re-layouts, per_device(): row_grads[None]  17.9 us
  transfers between devices with their start and end apart: 5, of which 5 were waited for; matrix products, arithmetic and copies ran while one was open for 5% of the time, Pallas kernels for 0%

commit v1 on v0

v1 whole, which is shorter than its diff:
```python
import jax
import jax.numpy as jnp
from jax import lax
from jax.experimental import pallas as pl
from jax.experimental.pallas import tpu as pltpu
from jax.sharding import PartitionSpec as P

MESH = pl.DeviceIdType.MESH
F32 = jnp.float32
BF16 = jnp.bfloat16

norm_eps = 1e-06
clip_limit = 0.5

RING = 4
GROUPS = 8
TROWS = 32
TILES = 4
CAP = 8
ROWS = 128
ALL_ROWS = GROUPS * ROWS
ENC = 3200
BLOCK = 200
PAIR = 2 * BLOCK
WIDTH = 1024
HALF = WIDTH // 2
KEYS = 512
SLOT_ROWS = CAP * TROWS
CHUNKS = 4
CHUNK = WIDTH // CHUNKS


def kernel(
    visual, projector, key_weight, gain, cotangent, residual, counts, offsets,
    grad_out, residual_out,
    v, vt, pj, pf, yv, u, k, kf, kw, cot, onehot, rg, res, qa, qb, ra, rb, ra2, rb2, wg, st,
    local_sem, out_sem,
    v_send, v_recv, k_send, k_recv, p_send, p_recv, s_send, s_recv,
    a_send, a_recv, b_send, b_recv, a2_send, a2_recv, b2_send, b2_recv,
):
    g, d = lax.axis_index("grp"), lax.axis_index("dp")
    x, c = lax.div(g, 2), lax.rem(g, 2)
    z, y = lax.div(d, RING), lax.rem(d, RING)
    s = 1 - 2 * c

    def step(at, n):
        return lax.rem(at + n + 2 * RING, RING)

    def grp_dev(n):
        return (step(x, n) * 2 + c, d)

    other = (x * 2 + 1 - c, d)

    def y_dev(n):
        return (g, z * RING + step(y, n))

    def z_dev(n):
        return (g, step(z, n) * RING + y)

    def remote(src, dst, send, recv, device):
        return pltpu.make_async_remote_copy(
            src, dst, send, recv, device_id=device, device_id_type=MESH
        )

    sent = []

    def start(src, dst, send, recv, device):
        copy = remote(src, dst, send, recv, device)
        copy.start()
        sent.append(copy)

    def arrived(dst, send, recv):
        remote(dst, dst, send, recv, other).wait_recv()

    own_rows = pl.ds(pl.multiple_of(g * ROWS, ROWS), ROWS)
    loads = [
        pltpu.make_async_copy(visual, v.at[own_rows], local_sem.at[0]),
        pltpu.make_async_copy(cotangent, cot, local_sem.at[1]),
        pltpu.make_async_copy(
            key_weight.at[pl.ds(pl.multiple_of(g * WIDTH, WIDTH), WIDTH)], kw, local_sem.at[2]
        ),
        pltpu.make_async_copy(residual, res, local_sem.at[3]),
    ]
    for n in range(CHUNKS):
        loads.append(
            pltpu.make_async_copy(
                projector.at[:, pl.ds(n * CHUNK, CHUNK)], pj.at[n, d], local_sem.at[4 + n]
            )
        )
    for load in loads:
        load.start()

    barrier = pltpu.get_barrier_semaphore()
    friends = [(lax.rem(g + n, GROUPS), d) for n in range(1, GROUPS)]
    friends += [y_dev(1), y_dev(-1), z_dev(1), z_dev(-1)]
    for friend in friends:
        pl.semaphore_signal(barrier, inc=1, device_id=friend, device_id_type=MESH)
    pl.semaphore_wait(barrier, len(friends))

    def x_slot(n, core):
        return step(x, n) * 2 + core

    class Gather:
        def __init__(self, buf, rows, send, recv):
            self.buf, self.rows, self.send, self.recv = buf, rows, send, recv

        def at(self, slot):
            return self.buf.at[pl.ds(pl.multiple_of(slot * self.rows, self.rows), self.rows)]

        def go(self, m, src_slot, device, src=None):
            here = self.at(src_slot)
            start(here if src is None else src, here, self.send.at[m], self.recv.at[m], device)

        def wait(self, m, slot):
            arrived(self.at(slot), self.send.at[m], self.recv.at[m])

        def own(self, src=None):
            self.go(0, g, grp_dev(s), src)
            self.go(1, g, grp_dev(-s), src)
            self.go(3, g, other, src)

        def near(self):
            self.wait(0, x_slot(-s, c))
            self.go(2, x_slot(-s, c), grp_dev(s))
            self.go(4, x_slot(-s, c), other)
            self.wait(1, x_slot(s, c))
            self.go(5, x_slot(s, c), other)

        def far(self):
            self.wait(2, x_slot(2, c))
            self.go(6, x_slot(2, c), other)

        def near_other(self):
            self.wait(3, x_slot(0, 1 - c))
            self.wait(4, x_slot(s, 1 - c))
            self.wait(5, x_slot(-s, 1 - c))

        def far_other(self):
            self.wait(6, x_slot(2, 1 - c))

    rows = Gather(v, ROWS, v_send, v_recv)
    keys = Gather(k, CAP, k_send, k_recv)

    rows.own(visual)

    def p_slot(n, first, second):
        if n % 2 == 0:
            return step(z, second) * RING + step(y, first)
        return step(z, first) * RING + step(y, second)

    def p_go(n, m, slot, device, src=None):
        here = pj.at[n, slot]
        start(here if src is None else src, here, p_send.at[n, m], p_recv.at[n, m], device)

    def p_wait(n, m, slot):
        arrived(pj.at[n, slot], p_send.at[n, m], p_recv.at[n, m])

    def first_dev(n, by):
        return y_dev(by) if n % 2 == 0 else z_dev(by)

    def second_dev(n, by):
        return z_dev(by) if n % 2 == 0 else y_dev(by)

    firsts = (0, -s, s, 2)

    def p_spread(n, j, src=None):
        slot = p_slot(n, firsts[j], 0)
        p_go(n, 3 + 3 * j, slot, second_dev(n, s), src)
        p_go(n, 4 + 3 * j, slot, second_dev(n, -s), src)

    def p_own(n):
        src = pj.at[n, d]
        p_go(n, 0, d, first_dev(n, s), src)
        p_go(n, 1, d, first_dev(n, -s), src)

    def p_first(n):
        p_wait(n, 0, p_slot(n, -s, 0))
        p_go(n, 2, p_slot(n, -s, 0), first_dev(n, s))

    def p_first_spread(n):
        p_spread(n, 1)
        p_wait(n, 1, p_slot(n, s, 0))
        p_spread(n, 2)
        p_wait(n, 2, p_slot(n, 2, 0))
        p_spread(n, 3)

    def p_second(n, j):
        p_wait(n, 3 + 3 * j, p_slot(n, firsts[j], -s))
        p_go(n, 5 + 3 * j, p_slot(n, firsts[j], -s), second_dev(n, s))

    def p_last(n):
        for j in range(RING):
            p_wait(n, 4 + 3 * j, p_slot(n, firsts[j], s))
            p_wait(n, 5 + 3 * j, p_slot(n, firsts[j], 2))

    for n in range(CHUNKS):
        loads[4 + n].wait()
        p_own(n)
    for n in range(CHUNKS):
        p_spread(n, 0)

    tiles = []
    earlier = [jnp.int32(0)] * GROUPS
    for source in range(GROUPS):
        route = [counts[source, b] for b in range(GROUPS)]
        first = [offsets[source, b] for b in range(GROUPS)]
        for t in range(TILES):
            target, slot, position = jnp.int32(0), jnp.int32(0), jnp.int32(0)
            passed = jnp.int32(0)
            for b in range(GROUPS):
                hit = (passed <= t) & (t < passed + route[b])
                within = t - passed
                target = jnp.where(hit, b, target)
                slot = jnp.where(hit, earlier[b] + within, slot)
                position = jnp.where(hit, first[b] + within * TROWS, position)
                passed = passed + route[b]
            slot = jnp.clip(slot, 0, CAP - 1)
            tiles.append((target, slot, position))
        earlier = [e + r for e, r in zip(earlier, route)]
    slot_iota = (
        lax.broadcasted_iota(jnp.int32, (TROWS, KEYS), 1)
        - lax.broadcasted_iota(jnp.int32, (TROWS, KEYS), 0)
    )
    for i in range(CAP):
        place = jnp.int32(-4096)
        for target, slot, position in tiles:
            place = jnp.where((target == g) & (slot == i), position, place)
        onehot[i * TROWS : (i + 1) * TROWS, :] = jnp.where(slot_iota == place, 1.0, 0.0).astype(BF16)
    loads[1].wait()
    k[pl.ds(g * CAP, CAP)] = jnp.dot(
        onehot[...], cot[...], preferred_element_type=F32
    ).astype(BF16).reshape(CAP, TROWS, KEYS)
    keys.own()

    def transpose(slot):
        @pl.loop(0, 5)
        def _(i):
            cols = pl.ds(pl.multiple_of(i * 640, 640), 640)
            block = v[pl.ds(pl.multiple_of(slot * ROWS, ROWS), ROWS), cols]
            vt[cols, pl.ds(pl.multiple_of(slot * ROWS, ROWS), ROWS)] = block.T

    def project(n):
        @pl.loop(0, 8)
        def _(i):
            low = pj[n, 2 * i].astype(F32)
            high = pj[n, 2 * i + 1].astype(F32)
            pf[pl.ds(pl.multiple_of(i * PAIR, PAIR), PAIR), :] = jnp.concatenate(
                [low, high], axis=0
            ).astype(BF16)

        @pl.loop(0, 2)
        def _(i):
            part = pl.ds(pl.multiple_of(i * 512, 512), 512)
            yv[part, n * CHUNK : (n + 1) * CHUNK] = jnp.dot(
                v[part, :], pf[...], preferred_element_type=F32
            ).astype(BF16)

    loads[0].wait()
    loads[2].wait()
    for n in range(CHUNKS):
        p_first(n)
    for n in range(CHUNKS):
        p_first_spread(n)
    transpose(g)
    for n in (0, 1):
        for j in range(RING):
            p_second(n, j)
    rows.near()
    for n in (2, 3):
        for j in (0, 1):
            p_second(n, j)
    keys.near()
    transpose(x_slot(-s, c))
    for n in (2, 3):
        for j in (2, 3):
            p_second(n, j)
    rows.far()
    transpose(x_slot(s, c))
    rows.near_other()
    transpose(x_slot(0, 1 - c))
    transpose(x_slot(-s, 1 - c))
    transpose(x_slot(s, 1 - c))
    transpose(x_slot(2, c))
    keys.far()
    rows.far_other()
    transpose(x_slot(2, 1 - c))
    for n in (0, 1):
        p_last(n)
        project(n)
    keys.near_other()
    keys.far_other()
    for i, (target, slot, _) in enumerate(tiles):
        kf[i * TROWS : (i + 1) * TROWS, :] = k[target * CAP + slot]
    gains = gain[pl.ds(g, 1), :]

    @pl.loop(0, 2)
    def _(i):
        part = pl.ds(pl.multiple_of(i * 512, 512), 512)
        u[part, :] = gains * lax.dot_general(
            kf[part, :], kw[...], (((1,), (1,)), ((), ())), preferred_element_type=F32
        )

    for n in (2, 3):
        p_last(n)
        project(n)

    for i in range(GROUPS):
        part = slice(i * ROWS, (i + 1) * ROWS)
        squares = jnp.zeros((ROWS, 128), F32)
        products = jnp.zeros((ROWS, 128), F32)
        for j in range(WIDTH // 128):
            cols = slice(j * 128, (j + 1) * 128)
            value = yv[part, cols].astype(F32)
            squares += value * value
            products += value * u[part, cols]
        st[g, pl.ds(i, 1), :] = jnp.sum(squares.T, axis=0, keepdims=True)
        st[g, pl.ds(GROUPS + i, 1), :] = jnp.sum(products.T, axis=0, keepdims=True)
    for n in range(1, GROUPS):
        start(st.at[g], st.at[g], s_send.at[n], s_recv.at[n], (lax.rem(g + n, GROUPS), d))
    for n in range(1, GROUPS):
        arrived(st.at[lax.rem(g - n + GROUPS, GROUPS)], s_send.at[n], s_recv.at[n])
    total = st[0]
    for n in range(1, GROUPS):
        total = total + st[n]
    mean = total * (1.0 / (GROUPS * WIDTH))
    inverse = lax.rsqrt(mean[:GROUPS] + norm_eps)
    inner = inverse * mean[GROUPS:]
    for i in range(GROUPS):
        part = slice(i * ROWS, (i + 1) * ROWS)
        inv = jnp.broadcast_to(inverse[i : i + 1], (ROWS, 128)).T
        inn = jnp.broadcast_to((inverse * inner)[i : i + 1], (ROWS, 128)).T
        for j in range(WIDTH // 128):
            cols = slice(j * 128, (j + 1) * 128)
            value = yv[part, cols].astype(F32)
            rg[part, cols] = (inv * (u[part, cols] - value * inn)).astype(BF16)

    loads[3].wait()
    lead_y = 1 - lax.div(y, 2)
    lead_z = 1 - lax.div(z, 2)

    def ordered(lead, i):
        return lax.rem(lead + i, 2)

    def unit(p, half):
        part = pl.ds(pl.multiple_of(p * PAIR, PAIR), PAIR)
        cols = slice(half * HALF, (half + 1) * HALF)
        term = jnp.dot(vt[part, :], rg[:, cols], preferred_element_type=F32)
        carried = term + res[part, cols].astype(F32)
        clipped = jnp.clip(carried, -clip_limit, clip_limit)
        res[part, cols] = (carried - clipped).astype(BF16)
        return clipped[:BLOCK].astype(BF16), clipped[BLOCK:].astype(BF16)

    def a_copy(m, i, by, device):
        return remote(
            qa.at[step(z, by) * 2 + ordered(lead_y, i)], ra.at[2 * m + i],
            a_send.at[m, i], a_recv.at[m, i], device,
        )

    def b_copy(m, i, by, device):
        return remote(
            qb.at[step(y, by) * 2 + ordered(lead_z, i)], rb.at[2 * m + i],
            b_send.at[m, i], b_recv.at[m, i], device,
        )

    @pl.loop(0, 8)
    def _(i):
        turn, which = lax.div(i, 2), lax.rem(i, 2)
        by = jnp.where(turn == 0, 2, jnp.where(turn == 1, -s, jnp.where(turn == 2, s, 0)))
        p = step(z, by) * 2 + ordered(lead_y, which)
        low, high = unit(p, 0)
        qa[p, 0] = low
        qa[p, 1] = high

        @pl.when(turn == 0)
        def _():
            a_copy(0, which, 2, z_dev(s)).start()

        @pl.when(turn == 1)
        def _():
            a_copy(1, which, -s, z_dev(-s)).start()

        pair = ordered(lead_y, lax.div(i, 4))
        plane = lax.rem(2 * lead_z + lax.rem(i, 4), RING)
        low, high = unit(plane * 2 + pair, 1)
        at = lax.div(plane, 2)
        qb[4 * pair + at, lax.rem(plane, 2)] = low
        qb[4 * pair + 2 + at, lax.rem(plane, 2)] = high

        @pl.when(i == 1)
        def _():
            b_copy(0, 0, 2, y_dev(s)).start()

        @pl.when(i == 3)
        def _():
            b_copy(0, 1, 2, y_dev(s)).start()

        @pl.when(i == 5)
        def _():
            b_copy(1, 0, -s, y_dev(-s)).start()

        @pl.when(i == 7)
        def _():
            b_copy(1, 1, -s, y_dev(-s)).start()

    store = pltpu.make_async_copy(res, residual_out, out_sem.at[0])
    store.start()

    def add(buf, index, terms):
        for j in range(2):
            value = buf[index, j].astype(F32)
            for term_buf, term_index in terms:
                value = value + term_buf[term_index, j].astype(F32)
            buf[index, j] = value.astype(BF16)

    for i in range(2):
        a_copy(0, i, 2, z_dev(s)).wait_recv()
        add(qa, step(z, s) * 2 + ordered(lead_y, i), [(ra, i)])
        a_copy(2, i, s, z_dev(s)).start()
        b_copy(0, i, 2, y_dev(s)).wait_recv()
        add(qb, step(y, s) * 2 + ordered(lead_z, i), [(rb, i)])
        b_copy(2, i, s, y_dev(s)).start()

    def a_block(by):
        yy = step(y, by)
        return (2 * z + lax.div(yy, 2), lax.rem(yy, 2))

    def b_block(by):
        zz = step(z, by)
        return (2 * y + lax.div(zz, 2), lax.rem(zz, 2))

    def a2_copy(m, by, device):
        return remote(qa.at[a_block(by)], ra2.at[m], a2_send.at[m], a2_recv.at[m], device)

    def b2_copy(m, by, device):
        return remote(qb.at[b_block(by)], rb2.at[m], b2_send.at[m], b2_recv.at[m], device)

    for i in range(2):
        for m in (1, 2):
            a_copy(m, i, 0, other).wait_recv()
            b_copy(m, i, 0, other).wait_recv()
        add(qa, 2 * z + ordered(lead_y, i), [(ra, 2 + i), (ra, 4 + i)])
        add(qb, 2 * y + ordered(lead_z, i), [(rb, 2 + i), (rb, 4 + i)])
        if i == 0:
            a2_copy(0, 2, y_dev(s)).start()
            b2_copy(0, 2, z_dev(s)).start()
    a2_copy(1, -s, y_dev(-s)).start()
    b2_copy(1, -s, z_dev(-s)).start()
    a2_copy(0, 2, y_dev(s)).wait_recv()
    qa[a_block(s)] = (qa[a_block(s)].astype(F32) + ra2[0].astype(F32)).astype(BF16)
    a2_copy(2, s, y_dev(s)).start()
    b2_copy(0, 2, z_dev(s)).wait_recv()
    qb[b_block(s)] = (qb[b_block(s)].astype(F32) + rb2[0].astype(F32)).astype(BF16)
    b2_copy(2, s, z_dev(s)).start()
    a2_copy(1, 0, other).wait_recv()
    a2_copy(2, 0, other).wait_recv()
    wg[:, :HALF] = qa[a_block(0)].astype(F32) + ra2[1].astype(F32) + ra2[2].astype(F32)
    b2_copy(1, 0, other).wait_recv()
    b2_copy(2, 0, other).wait_recv()
    wg[:, HALF:] = qb[b_block(0)].astype(F32) + rb2[1].astype(F32) + rb2[2].astype(F32)
    last = pltpu.make_async_copy(wg, grad_out, out_sem.at[1])
    last.start()

    for copy in sent:
        copy.wait_send()
    for i in range(2):
        for m, by in enumerate((2, -s, s)):
            a_copy(m, i, by, other).wait_send()
            b_copy(m, i, by, other).wait_send()
    for m, by in enumerate((2, -s, s)):
        a2_copy(m, by, other).wait_send()
        b2_copy(m, by, other).wait_send()
    store.wait()
    last.wait()


def per_device(visual, projector, key_weight, norm_gain, cotangent, residual, counts, offsets):
    gain = norm_gain.astype(F32).reshape(GROUPS, WIDTH)
    anywhere = pl.BlockSpec(memory_space=pl.ANY)
    scalars = pl.BlockSpec(memory_space=pltpu.SMEM)
    dma = pltpu.SemaphoreType.DMA
    return pl.pallas_call(
        kernel,
        out_shape=(
            jax.ShapeDtypeStruct((BLOCK, WIDTH), F32),
            jax.ShapeDtypeStruct((ENC, WIDTH), BF16),
        ),
        in_specs=[
            anywhere, anywhere, anywhere, pl.BlockSpec(memory_space=pltpu.VMEM), anywhere, anywhere,
            scalars, scalars,
        ],
        out_specs=(anywhere, anywhere),
        scratch_shapes=[
            pltpu.VMEM((ALL_ROWS, ENC), BF16),
            pltpu.VMEM((ENC, ALL_ROWS), BF16),
            pltpu.VMEM((CHUNKS, 16, BLOCK, CHUNK), BF16),
            pltpu.VMEM((ENC, CHUNK), BF16),
            pltpu.VMEM((ALL_ROWS, WIDTH), BF16),
            pltpu.VMEM((ALL_ROWS, WIDTH), F32),
            pltpu.VMEM((GROUPS * CAP, TROWS, KEYS), BF16),
            pltpu.VMEM((ALL_ROWS, KEYS), BF16),
            pltpu.VMEM((WIDTH, KEYS), BF16),
            pltpu.VMEM((512, KEYS), BF16),
            pltpu.VMEM((SLOT_ROWS, 512), BF16),
            pltpu.VMEM((ALL_ROWS, WIDTH), BF16),
            pltpu.VMEM((ENC, WIDTH), BF16),
            pltpu.VMEM((8, 2, BLOCK, HALF), BF16),
            pltpu.VMEM((8, 2, BLOCK, HALF), BF16),
            pltpu.VMEM((6, 2, BLOCK, HALF), BF16),
            pltpu.VMEM((6, 2, BLOCK, HALF), BF16),
            pltpu.VMEM((3, BLOCK, HALF), BF16),
            pltpu.VMEM((3, BLOCK, HALF), BF16),
            pltpu.VMEM((BLOCK, WIDTH), F32),
            pltpu.VMEM((GROUPS, 2 * GROUPS, 128), F32),
            dma((8,)), dma((2,)),
            dma((7,)), dma((7,)), dma((7,)), dma((7,)),
            dma((CHUNKS, 15)), dma((CHUNKS, 15)), dma((GROUPS,)), dma((GROUPS,)),
            dma((3, 2)), dma((3, 2)), dma((3, 2)), dma((3, 2)),
            dma((3,)), dma((3,)), dma((3,)), dma((3,)),
        ],
        compiler_params=pltpu.CompilerParams(
            collective_id=0, has_side_effects=True, vmem_limit_bytes=62 * 2**20
        ),
        cost_estimate=pl.CostEstimate(flops=16 * 10**9, bytes_accessed=20 * 10**6, transcendentals=0),
    )(
        visual[0], projector, key_weight, gain, cotangent[0], residual, counts[0], offsets[0]
    )


def solution(mesh):
    placed = (
        P("dp", "grp", None),
        P("dp", "grp"),
        P(),
        P(),
        P("dp", "grp", None),
        P("dp", "grp"),
        P("dp", None, None),
        P("dp", None, None),
    )
    return jax.shard_map(
        per_device,
        mesh=mesh,
        in_specs=placed,
        out_specs=(P("dp", "grp"), P("dp", "grp")),
        check_vma=False,
    )
```

time: 524 us -> 116 us (0.22)
  waiting for transfers between devices: 306 us -> 0 us
  Pallas kernels: 0 us -> 104 us
  local copies, waits for them, and re-layouts: 88.3 us -> 9.85 us
  other arithmetic: 65.2 us -> 0 us
  matrix products: 37.8 us -> 0 us
  between operations: 14.6 us -> 0.64 us
  starting transfers between devices: 9.63 us -> 0 us
    unnamed x4 -> x0, waiting for transfers between devices: 113 us -> none
    all_gather x2 -> x0, waiting for transfers between devices: 106 us -> none  [the longest x1 64.8 us: per_device(): lax.all_gather(projector, 'dp', axis=0, tiled=True)]
    pallas_call x0 -> x1, Pallas kernels: none -> 104 us  [per_device(): pl.pallas_call(kernel, out_shape=(jax.ShapeDtypeStruct((BLOCK, WIDTH), F3...]
    all_to_all x2 -> x0, waiting for transfers between devices: 87.5 us -> none  [the longest x1 48 us: per_device(): lax.all_to_all(outgoing, 'grp', split_axis=0, concat_axis=2, tiled=True)]
    unnamed x2 -> x0, other arithmetic: 46.8 us -> none
    dot_general x3 -> x0, matrix products: 37.8 us -> none  [the longest x1 15.4 us: per_device(): lax.dot_general(gathered, row_grad, (((0,), (0,)), ((), ())), preferred_e...]
    unnamed x17 -> x2, local copies, waits for them, and re-layouts: 44.8 us -> 8.51 us
    gather x3 -> x0, local copies, waits for them, and re-layouts: 18.5 us -> none  [the longest x1 9.61 us: per_device(): jnp.take(projected, row_index, axis=0).reshape(groups, length, block_width)]
  transfers between devices with their start and end apart: 5 -> 0, of which waited for: 5 -> 0; matrix products, arithmetic and copies ran while one was open for 5% -> 0% of each run, Pallas kernels for 0% -> 0%
where the time goes in v1:
time: 116 us; the launch traced here: 115 us
  Pallas kernels  104 us (90%)
  local copies, waits for them, and re-layouts  9.85 us (8%)
    pallas_call x1, Pallas kernels, per_device(): pl.pallas_call(kernel, out_shape=(jax.ShapeDtypeStruct((BLOCK, WIDTH), F3...  104 us
    unnamed x2, local copies, waits for them, and re-layouts  8.51 us

profile of v1, /device:TPU:0, one launch (start us, length us, event | category | flops | bytes accessed | tf_op | source)
XLA Modules:
  0.0 114.8 jit_solution(16434676300244844361)
XLA Ops:
  0.6 1.3 %reshape.12.gain = f32[8,1024]{1,0:T(8,128)} reshape(bf16[8192]{0:T(1024)(128)(2,1)} %param.11) | data formatting | bytes 49152 | tf_op jit(solution)/shard_map/reshape | solution.py:477
  2.0 104.3 %shard_map.95 = (f32[200,1024]{1,0:T(8,128)}, bf16[3200,1024]{1,0:T(8,128)(2,1)}) custom-call(bf16[128,3200]{1,0:T(8,128)(2,1)} %bitcast.4, bf16[200,1024]{1,0:T(8,128)(2,1)} %projector.1, bf16[8192,512]{1,0:T(8,128)(2,1)} %key_weight.1, f32[8,1024]{1,0:T(8,128)} %reshape.12.gain, bf16[512,512]{1,0:T(8,128)(2,1)} %bitcast.5, bf16[3200,1024]{1,0:T(8,128)(2,1)} %residual.1, ...), custom_call_target="tpu_custom_call" | custom-call | flops 16000000000 | bytes 20000000 | tf_op jit(solution)/shard_map/pallas_call | solution.py:481
  106.2 2.1 %copy.12 = f32[200,1024]{1,0:T(8,128)} copy(f32[200,1024]{1,0:T(8,128)} %get-tuple-element.4) | data formatting | bytes 1638400
  108.4 6.4 %copy.13 = bf16[3200,1024]{1,0:T(8,128)(2,1)} copy(bf16[3200,1024]{1,0:T(8,128)(2,1)} %get-tuple-element.5) | data formatting | bytes 13107200

commit v2 on v1

v2 whole, which is shorter than its diff:
```python
import jax
import jax.numpy as jnp
from jax import lax
from jax.experimental import pallas as pl
from jax.experimental.pallas import tpu as pltpu
from jax.sharding import PartitionSpec as P

MESH = pl.DeviceIdType.MESH
F32 = jnp.float32
BF16 = jnp.bfloat16

norm_eps = 1e-06
clip_limit = 0.5

RING = 4
GROUPS = 8
TROWS = 32
TILES = 4
CAP = 8
ROWS = 128
ALL_ROWS = GROUPS * ROWS
ENC = 3200
BLOCK = 200
PAIR = 2 * BLOCK
WIDTH = 1024
HALF = WIDTH // 2
PARTS = ((0, 256), (256, 256))
KEYS = 512
SLOT_ROWS = CAP * TROWS
CHUNKS = 4
WIDE, NARROW = 384, 128
ROW_PIECES, KEY_PIECES = 4, 2


def kernel(
    visual, projector, key_weight, gain, cotangent, residual, counts, offsets,
    wg, res,
    v, vt, wide, narrow, pf, yv, u, k, kf, kw, cot, onehot, rg, gains, st,
    qa0, qa1, qb0, qb1, ra0, ra1, rb0, rb1, ra20, ra21, rb20, rb21,
    local_sem,
    v_send, v_recv, v_other, k_send, k_recv, k_other, p_send, p_recv, p_end, s_send, s_recv,
    q_send, q_long, q_near, q2_send, q2_long, q2_near,
):
    g, d = lax.axis_index("grp"), lax.axis_index("dp")
    x, c = lax.div(g, 2), lax.rem(g, 2)
    z, y = lax.div(d, RING), lax.rem(d, RING)
    s = 1 - 2 * c

    def step(at, n):
        return lax.rem(at + n + 2 * RING, RING)

    def grp_dev(n):
        return (step(x, n) * 2 + c, d)

    other = (x * 2 + 1 - c, d)

    def y_dev(n):
        return (g, z * RING + step(y, n))

    def z_dev(n):
        return (g, step(z, n) * RING + y)

    def remote(src, dst, send, recv, device):
        return pltpu.make_async_remote_copy(
            src, dst, send, recv, device_id=device, device_id_type=MESH
        )

    def start(src, dst, send, recv, device):
        remote(src, dst, send, recv, device).start()

    def done(like, sem):
        pltpu.make_async_copy(like, like, sem).wait()

    own_rows = pl.ds(pl.multiple_of(g * ROWS, ROWS), ROWS)
    loads = [
        pltpu.make_async_copy(visual, v.at[own_rows], local_sem.at[0]),
        pltpu.make_async_copy(cotangent, cot, local_sem.at[1]),
        pltpu.make_async_copy(
            key_weight.at[pl.ds(pl.multiple_of(g * WIDTH, WIDTH), WIDTH)], kw, local_sem.at[2]
        ),
        pltpu.make_async_copy(residual, res, local_sem.at[3]),
    ]

    def chunk_cols(n):
        return (n * WIDE, WIDE) if n < 2 else (2 * WIDE + (n - 2) * NARROW, NARROW)

    def pj(n, slot):
        return wide.at[n, slot] if n < 2 else narrow.at[n - 2, slot]

    for n in range(CHUNKS):
        loads.append(
            pltpu.make_async_copy(
                projector.at[:, pl.ds(*chunk_cols(n))], pj(n, d), local_sem.at[4 + n]
            )
        )
    loads.append(
        pltpu.make_async_copy(
            gain.at[pl.ds(pl.multiple_of(g * WIDTH, WIDTH), WIDTH)], gains, local_sem.at[8]
        )
    )
    for load in loads:
        load.start()

    barrier = pltpu.get_barrier_semaphore()
    friends = [(lax.rem(g + n, GROUPS), d) for n in range(1, GROUPS)]
    friends += [y_dev(1), y_dev(-1), z_dev(1), z_dev(-1)]
    for friend in friends:
        pl.semaphore_signal(barrier, inc=1, device_id=friend, device_id_type=MESH)
    pl.semaphore_wait(barrier, len(friends))

    def x_slot(n, core):
        return step(x, n) * 2 + core

    class Gather:
        def __init__(self, buf, rows, pieces, send, recv, other_recv):
            self.buf, self.rows, self.send, self.recv = buf, rows, send, recv
            self.other = other_recv
            self.pieces, self.piece = pieces, rows // pieces

        def at(self, slot, i):
            row = pl.multiple_of(slot * self.rows + i * self.piece, self.piece)
            return self.buf.at[pl.ds(row, self.piece)]

        def go(self, m, i, slot, device):
            here = self.at(slot, i)
            start(here, here, self.send, self.recv.at[m, i], device)

        def give(self, m, i, slot):
            here = self.at(slot, i)
            start(here, here, self.send, self.other.at[m], other)

        def own(self, i):
            self.go(0, i, g, grp_dev(s))
            self.go(1, i, g, grp_dev(-s))

        def own_other(self, i):
            self.give(0, i, g)

        def near(self, i):
            done(self.at(x_slot(-s, c), i), self.recv.at[0, i])
            self.go(2, i, x_slot(-s, c), grp_dev(s))
            self.give(1, i, x_slot(-s, c))
            done(self.at(x_slot(s, c), i), self.recv.at[1, i])
            self.give(2, i, x_slot(s, c))

        def far(self, i):
            done(self.at(x_slot(2, c), i), self.recv.at[2, i])
            self.give(3, i, x_slot(2, c))

        def from_other(self, m):
            done(self.buf.at[pl.ds(0, self.rows)], self.other.at[m])

    rows = Gather(v, ROWS, ROW_PIECES, v_send.at[0], v_recv, v_other)
    keys = Gather(k, CAP, KEY_PIECES, k_send.at[0], k_recv, k_other)

    loads[0].wait()
    for i in range(ROW_PIECES):
        rows.own(i)

    def p_slot(n, first, second):
        if n % 2 == 0:
            return step(z, second) * RING + step(y, first)
        return step(z, first) * RING + step(y, second)

    def p_go(n, recv, slot, device):
        start(pj(n, slot), pj(n, slot), p_send.at[n], recv, device)

    def p_wait(n, m, slot):
        done(pj(n, slot), p_recv.at[n, m])

    def first_dev(n, by):
        return y_dev(by) if n % 2 == 0 else z_dev(by)

    def second_dev(n, by):
        return z_dev(by) if n % 2 == 0 else y_dev(by)

    firsts = (0, -s, s, 2)

    def p_spread(n, j):
        slot = p_slot(n, firsts[j], 0)
        p_go(n, p_recv.at[n, 3 + j], slot, second_dev(n, s))
        p_go(n, p_end.at[n], slot, second_dev(n, -s))

    def p_own(n):
        p_go(n, p_recv.at[n, 0], d, first_dev(n, s))
        p_go(n, p_recv.at[n, 1], d, first_dev(n, -s))

    def p_first(n):
        p_wait(n, 0, p_slot(n, -s, 0))
        p_go(n, p_recv.at[n, 2], p_slot(n, -s, 0), first_dev(n, s))

    def p_first_spread(n):
        p_spread(n, 1)
        p_wait(n, 1, p_slot(n, s, 0))
        p_spread(n, 2)
        p_wait(n, 2, p_slot(n, 2, 0))
        p_spread(n, 3)

    def p_second(n, j):
        p_wait(n, 3 + j, p_slot(n, firsts[j], -s))
        p_go(n, p_end.at[n], p_slot(n, firsts[j], -s), second_dev(n, s))

    def p_slots(n, count):
        return wide.at[n, pl.ds(0, count)] if n < 2 else narrow.at[n - 2, pl.ds(0, count)]

    def p_last(n):
        done(p_slots(n, 8), p_end.at[n])

    for n in range(CHUNKS):
        loads[4 + n].wait()
        p_own(n)

    tiles = []
    earlier = [jnp.int32(0)] * GROUPS
    for source in range(GROUPS):
        route = [counts[source, b] for b in range(GROUPS)]
        first = [offsets[source, b] for b in range(GROUPS)]
        for t in range(TILES):
            target, slot, position = jnp.int32(0), jnp.int32(0), jnp.int32(0)
            passed = jnp.int32(0)
            for b in range(GROUPS):
                hit = (passed <= t) & (t < passed + route[b])
                within = t - passed
                target = jnp.where(hit, b, target)
                slot = jnp.where(hit, earlier[b] + within, slot)
                position = jnp.where(hit, first[b] + within * TROWS, position)
                passed = passed + route[b]
            slot = jnp.clip(slot, 0, CAP - 1)
            tiles.append((target, slot, position))
        earlier = [e + r for e, r in zip(earlier, route)]
    slot_iota = (
        lax.broadcasted_iota(jnp.int32, (TROWS, KEYS), 1)
        - lax.broadcasted_iota(jnp.int32, (TROWS, KEYS), 0)
    )
    for i in range(CAP):
        place = jnp.int32(-4096)
        for target, slot, position in tiles:
            place = jnp.where((target == g) & (slot == i), position, place)
        onehot[i * TROWS : (i + 1) * TROWS, :] = jnp.where(slot_iota == place, 1.0, 0.0).astype(BF16)
    loads[1].wait()
    k[pl.ds(g * CAP, CAP)] = jnp.dot(
        onehot[...], cot[...], preferred_element_type=F32
    ).astype(BF16).reshape(CAP, TROWS, KEYS)
    def transpose(slot):
        @pl.loop(0, 5)
        def _(i):
            cols = pl.ds(pl.multiple_of(i * 640, 640), 640)
            block = v[pl.ds(pl.multiple_of(slot * ROWS, ROWS), ROWS), cols]
            vt[cols, pl.ds(pl.multiple_of(slot * ROWS, ROWS), ROWS)] = block.T

    def assemble(pair):
        bufs, width = ((wide, WIDE), (narrow, NARROW))[pair]

        @pl.loop(0, 8)
        def _(i):
            part = pl.ds(pl.multiple_of(i * PAIR, PAIR), PAIR)
            for n in range(2):
                both = [bufs[n, 2 * i].astype(F32), bufs[n, 2 * i + 1].astype(F32)]
                pf[part, n * width : (n + 1) * width] = jnp.concatenate(both, axis=0).astype(BF16)

    def project(pair, i):
        first, last = ((0, 2 * WIDE), (2 * WIDE, WIDTH))[pair]
        part = slice(i * 512, (i + 1) * 512)
        yv[part, first:last] = jnp.dot(
            v[part, :], pf[:, : last - first], preferred_element_type=F32
        ).astype(BF16)

    for n in (0, 1):
        p_first(n)
    for n in (0, 1):
        p_spread(n, 0)
    for i in range(ROW_PIECES):
        rows.own_other(i)
    for n in (2, 3):
        p_first(n)
    for n in (0, 1):
        p_first_spread(n)
    for n in (2, 3):
        p_spread(n, 0)
    rows.near(0)
    for n in (2, 3):
        p_first_spread(n)
    transpose(g)
    for n in (0, 1):
        p_second(n, 0)
    rows.near(1)
    rows.from_other(0)
    transpose(x_slot(0, 1 - c))
    rows.near(2)
    for i in range(KEY_PIECES):
        keys.own(i)
        keys.own_other(i)
    for n in (0, 1):
        p_second(n, 1)
    rows.near(3)
    for n in (0, 1):
        p_second(n, 2)
    transpose(x_slot(-s, c))
    rows.far(0)
    transpose(x_slot(s, c))
    rows.far(1)
    for n in (0, 1):
        p_second(n, 3)
    rows.from_other(1)
    transpose(x_slot(s, 1 - c))
    rows.far(2)
    rows.from_other(2)
    transpose(x_slot(-s, 1 - c))
    rows.far(3)
    for n in (2, 3):
        for j in (0, 1):
            p_second(n, j)
    transpose(x_slot(2, c))
    for n in (0, 1):
        p_last(n)
    assemble(0)
    for n in (2, 3):
        for j in (2, 3):
            p_second(n, j)
    keys.near(0)
    rows.from_other(3)
    project(0, 0)
    keys.near(1)
    project(0, 1)
    keys.far(0)
    for n in (2, 3):
        p_last(n)
    assemble(1)
    project(1, 0)
    keys.far(1)
    project(1, 1)
    for m in range(4):
        keys.from_other(m)
    for i, (target, slot, _) in enumerate(tiles):
        kf[i * TROWS : (i + 1) * TROWS, :] = k[target * CAP + slot]
    loads[2].wait()
    loads[8].wait()
    gain_row = gains[...].astype(F32).reshape(1, WIDTH)
    for i in range(2):
        part = slice(i * 512, (i + 1) * 512)
        u[part, :] = gain_row * lax.dot_general(
            kf[part, :], kw[...], (((1,), (1,)), ((), ())), preferred_element_type=F32
        )

    for i in range(GROUPS):
        part = slice(i * ROWS, (i + 1) * ROWS)
        squares = jnp.zeros((ROWS, 128), F32)
        products = jnp.zeros((ROWS, 128), F32)
        for j in range(WIDTH // 128):
            cols = slice(j * 128, (j + 1) * 128)
            value = yv[part, cols].astype(F32)
            squares += value * value
            products += value * u[part, cols]
        st[g, pl.ds(i, 1), :] = jnp.sum(squares.T, axis=0, keepdims=True)
        st[g, pl.ds(GROUPS + i, 1), :] = jnp.sum(products.T, axis=0, keepdims=True)
    for n in range(1, GROUPS):
        start(st.at[g], st.at[g], s_send.at[0], s_recv.at[0], (lax.rem(g + n, GROUPS), d))
    transpose(x_slot(2, 1 - c))
    done(st.at[pl.ds(0, GROUPS - 1)], s_recv.at[0])
    total = st[0]
    for n in range(1, GROUPS):
        total = total + st[n]
    mean = total * (1.0 / (GROUPS * WIDTH))
    inverse = lax.rsqrt(mean[:GROUPS] + norm_eps)
    inner = inverse * mean[GROUPS:]
    for i in range(GROUPS):
        part = slice(i * ROWS, (i + 1) * ROWS)
        inv = jnp.broadcast_to(inverse[i : i + 1], (ROWS, 128)).T
        inn = jnp.broadcast_to((inverse * inner)[i : i + 1], (ROWS, 128)).T
        for j in range(WIDTH // 128):
            cols = slice(j * 128, (j + 1) * 128)
            value = yv[part, cols].astype(F32)
            rg[part, cols] = (inv * (u[part, cols] - value * inn)).astype(BF16)

    loads[3].wait()
    lead_y = 1 - lax.div(y, 2)
    lead_z = 1 - lax.div(z, 2)

    def unit(p, first, width):
        part = pl.ds(pl.multiple_of(p * PAIR, PAIR), PAIR)
        cols = slice(first, first + width)
        term = jnp.dot(vt[part, :], rg[:, cols], preferred_element_type=F32)
        carried = term + res[part, cols].astype(F32)
        clipped = jnp.clip(carried, -clip_limit, clip_limit)
        res[part, cols] = (carried - clipped).astype(BF16)
        return clipped[:BLOCK].astype(BF16), clipped[BLOCK:].astype(BF16)

    class Sum:
        def __init__(self, n, q, r, r2, at, near, lead, at2, near2):
            self.n, self.q, self.r, self.r2 = n, q, r, r2
            self.at, self.near, self.lead, self.at2, self.near2 = at, near, lead, at2, near2

        def piece(self, by, i):
            return 2 * step(self.at, by) + lax.rem(self.lead + i, 2)

        def send(self, m, i, by, to):
            recv = q_long.at[self.n, i] if m == 0 else q_near.at[self.n, i]
            start(
                self.q.at[self.piece(by, i)], self.r.at[2 * i + m - 1 if m else 4 + i],
                q_send.at[self.n], recv, self.near(to),
            )

        def long(self, i):
            self.send(0, i, 2, s)

        def plain(self, i):
            self.send(1, i, -s, -s)

        def middle(self, i):
            done(self.r.at[4 + i], q_long.at[self.n, i])
            self.add(self.piece(s, i), (4 + i,))
            self.send(2, i, s, s)

        def own(self, i):
            done(self.r.at[pl.ds(2 * i, 2)], q_near.at[self.n, i])
            self.add(self.piece(0, i), (2 * i, 2 * i + 1))

        def add(self, index, terms):
            for j in range(2):
                value = self.q[index, j].astype(F32)
                for term in terms:
                    value = value + self.r[term, j].astype(F32)
                self.q[index, j] = value.astype(BF16)

        def block(self, by):
            at2 = step(self.at2, by)
            return (2 * self.at + lax.div(at2, 2), lax.rem(at2, 2))

        def send2(self, m, by, to):
            recv = q2_long.at[self.n] if m == 0 else q2_near.at[self.n]
            start(
                self.q.at[self.block(by)], self.r2.at[(2, 0, 1)[m]],
                q2_send.at[self.n], recv, self.near2(to),
            )

        def long2(self):
            self.send2(0, 2, s)

        def plain2(self):
            self.send2(1, -s, -s)

        def middle2(self):
            done(self.r2.at[2], q2_long.at[self.n])
            here = self.block(s)
            self.q[here] = (self.q[here].astype(F32) + self.r2[2].astype(F32)).astype(BF16)
            self.send2(2, s, s)

        def finish(self, cols):
            done(self.r2.at[pl.ds(0, 2)], q2_near.at[self.n])
            total = self.q[self.block(0)].astype(F32) + self.r2[0].astype(F32)
            wg[:, cols] = total + self.r2[1].astype(F32)

        def sent(self):
            done(self.r, q_send.at[self.n])
            done(self.r2, q2_send.at[self.n])

    sums = []
    for n, (q_a, r_a, r2_a, q_b, r_b, r2_b) in enumerate(
        ((qa0, ra0, ra20, qb0, rb0, rb20), (qa1, ra1, ra21, qb1, rb1, rb21))
    ):
        sums.append(
            (
                Sum(2 * n, q_a, r_a, r2_a, z, z_dev, lead_y, y, y_dev),
                Sum(2 * n + 1, q_b, r_b, r2_b, y, y_dev, lead_z, z, z_dev),
            )
        )

    for (a, b), (first, width) in zip(sums, PARTS):

        @pl.loop(0, 8)
        def _(i):
            turn, which = lax.div(i, 2), lax.rem(i, 2)
            by = jnp.where(turn == 0, 2, jnp.where(turn == 1, -s, jnp.where(turn == 2, s, 0)))
            p = 2 * step(z, by) + lax.rem(lead_y + which, 2)
            low, high = unit(p, first, width)
            a.q[p, 0] = low
            a.q[p, 1] = high
            pair = lax.rem(lead_y + lax.div(i, 4), 2)
            plane = lax.rem(2 * lead_z + lax.rem(i, 4), RING)
            for n in range(2):
                pl.when(i == n)(lambda n=n: a.long(n))
                pl.when(i == 2 + n)(lambda n=n: a.plain(n))
            low, high = unit(2 * plane + pair, HALF + first, width)
            b.q[4 * pair + lax.div(plane, 2), lax.rem(plane, 2)] = low
            b.q[4 * pair + 2 + lax.div(plane, 2), lax.rem(plane, 2)] = high
            for n in range(2):
                pl.when(i == 1 + 2 * n)(lambda n=n: b.long(n))
                pl.when(i == 5 + 2 * n)(lambda n=n: b.plain(n))

    for pair in sums:
        for i in range(2):
            for part in pair:
                part.middle(i)
    for pair in sums:
        for i in range(2):
            for part in pair:
                part.own(i)
                if i == 0:
                    part.long2()
        for part in pair:
            part.plain2()
    for pair in sums:
        for part in pair:
            part.middle2()
    for (a, b), (first, width) in zip(sums, PARTS):
        a.finish(slice(first, first + width))
        b.finish(slice(HALF + first, HALF + first + width))

    done(v.at[pl.ds(0, 7 * ROWS)], v_send.at[0])
    done(k.at[pl.ds(0, 7 * CAP)], k_send.at[0])
    for n in range(CHUNKS):
        done(p_slots(n, 15), p_send.at[n])
    done(st.at[pl.ds(0, GROUPS - 1)], s_send.at[0])
    for pair in sums:
        for part in pair:
            part.sent()


def per_device(visual, projector, key_weight, norm_gain, cotangent, residual, counts, offsets):
    anywhere = pl.BlockSpec(memory_space=pl.ANY)
    scalars = pl.BlockSpec(memory_space=pltpu.SMEM)
    dma = pltpu.SemaphoreType.DMA
    return pl.pallas_call(
        kernel,
        out_shape=(
            pltpu.VMEM((BLOCK, WIDTH), F32),
            pltpu.VMEM((ENC, WIDTH), BF16),
        ),
        in_specs=[
            anywhere, anywhere, anywhere, anywhere, anywhere, anywhere, scalars, scalars,
        ],
        out_specs=(pl.BlockSpec(memory_space=pltpu.VMEM),) * 2,
        scratch_shapes=[
            pltpu.VMEM((ALL_ROWS, ENC), BF16),
            pltpu.VMEM((ENC, ALL_ROWS), BF16),
            pltpu.VMEM((2, 16, BLOCK, WIDE), BF16),
            pltpu.VMEM((2, 16, BLOCK, NARROW), BF16),
            pltpu.VMEM((ENC, 2 * WIDE), BF16),
            pltpu.VMEM((ALL_ROWS, WIDTH), BF16),
            pltpu.VMEM((ALL_ROWS, WIDTH), F32),
            pltpu.VMEM((GROUPS * CAP, TROWS, KEYS), BF16),
            pltpu.VMEM((ALL_ROWS, KEYS), BF16),
            pltpu.VMEM((WIDTH, KEYS), BF16),
            pltpu.VMEM((512, KEYS), BF16),
            pltpu.VMEM((SLOT_ROWS, 512), BF16),
            pltpu.VMEM((ALL_ROWS, WIDTH), BF16),
            pltpu.VMEM((WIDTH,), BF16),
            pltpu.VMEM((GROUPS, 2 * GROUPS, 128), F32),
            *[pltpu.VMEM((8, 2, BLOCK, w), BF16) for _, w in PARTS],
            *[pltpu.VMEM((8, 2, BLOCK, w), BF16) for _, w in PARTS],
            *[pltpu.VMEM((6, 2, BLOCK, w), BF16) for _, w in PARTS],
            *[pltpu.VMEM((6, 2, BLOCK, w), BF16) for _, w in PARTS],
            *[pltpu.VMEM((3, BLOCK, w), BF16) for _, w in PARTS],
            *[pltpu.VMEM((3, BLOCK, w), BF16) for _, w in PARTS],
            dma((9,)),
            dma((1,)), dma((3, ROW_PIECES)), dma((4,)),
            dma((1,)), dma((3, KEY_PIECES)), dma((4,)),
            dma((CHUNKS,)), dma((CHUNKS, 7)), dma((CHUNKS,)), dma((1,)), dma((1,)),
            dma((4,)), dma((4, 2)), dma((4, 2)), dma((4,)), dma((4,)), dma((4,)),
        ],
        compiler_params=pltpu.CompilerParams(
            collective_id=0, has_side_effects=True, vmem_limit_bytes=54 * 2**20
        ),
        cost_estimate=pl.CostEstimate(flops=16 * 10**9, bytes_accessed=20 * 10**6, transcendentals=0),
    )(
        visual[0], projector, key_weight, norm_gain, cotangent[0], residual, counts[0], offsets[0]
    )


def solution(mesh):
    placed = (
        P("dp", "grp", None),
        P("dp", "grp"),
        P(),
        P(),
        P("dp", "grp", None),
        P("dp", "grp"),
        P("dp", None, None),
        P("dp", None, None),
    )
    return jax.shard_map(
        per_device,
        mesh=mesh,
        in_specs=placed,
        out_specs=(P("dp", "grp"), P("dp", "grp")),
        check_vma=False,
    )
```

time: 116 us -> 106 us (0.914); the launches traced: 115 us -> 106 us
  local copies, waits for them, and re-layouts: 9.85 us -> 3.68 us
  Pallas kernels: 104 us -> 102 us
    unnamed x2, local copies, waits for them, and re-layouts: 8.51 us -> 3.68 us
    pallas_call x1, Pallas kernels: 104 us -> 102 us  [per_device(): pl.pallas_call(kernel, out_shape=(pltpu.VMEM((BLOCK, WIDTH), F32), pltpu....]
    reshape x1 -> x0, local copies, waits for them, and re-layouts: 1.34 us -> none  [per_device(): gain = norm_gain.astype(F32).reshape(GROUPS, WIDTH)]
where the time goes in v2:
time: 106 us
  Pallas kernels  102 us (96%)
  local copies, waits for them, and re-layouts  3.68 us (3%)
    pallas_call x1, Pallas kernels, per_device(): pl.pallas_call(kernel, out_shape=(pltpu.VMEM((BLOCK, WIDTH), F32), pltpu....  102 us
    unnamed x2, local copies, waits for them, and re-layouts  3.68 us

profile of v2, /device:TPU:0, one launch (start us, length us, event | category | flops | bytes accessed | tf_op | source)
XLA Modules:
  0.0 106.2 jit_solution(5900104838378316297)
XLA Ops:
  0.6 101.9 %shard_map.95 = (f32[200,1024]{1,0:T(8,128)S(1)}, bf16[3200,1024]{1,0:T(8,128)(2,1)S(1)}) custom-call(bf16[128,3200]{1,0:T(8,128)(2,1)} %bitcast.4, bf16[200,1024]{1,0:T(8,128)(2,1)} %projector.1, bf16[8192,512]{1,0:T(8,128)(2,1)} %key_weight.1, bf16[8192]{0:T(1024)(128)(2,1)} %gain.1, bf16[512,512]{1,0:T(8,128)(2,1)} %bitcast.5, ...), custom_call_target="tpu_custom_call" | custom-call | flops 16000000000 | bytes 20000000 | tf_op jit(solution)/shard_map/pallas_call | solution.py:523
  102.5 0.9 copy.12
  103.4 2.8 %copy.13 = bf16[3200,1024]{1,0:T(8,128)(2,1)} copy(bf16[3200,1024]{1,0:T(8,128)(2,1)S(1)} %get-tuple-element.3) | data formatting | bytes 13107200

commit v3 on v2

--- a/solution.py
+++ b/solution.py
@@ -24,18 +24,19 @@
 PAIR = 2 * BLOCK
 WIDTH = 1024
 HALF = WIDTH // 2
-PARTS = ((0, 256), (256, 256))
+PARTS = ((0, 384), (384, 128))
 KEYS = 512
 SLOT_ROWS = CAP * TROWS
 CHUNKS = 4
 WIDE, NARROW = 384, 128
 ROW_PIECES, KEY_PIECES = 4, 2
+WRITES = 8
 
 
 def kernel(
     visual, projector, key_weight, gain, cotangent, residual, counts, offsets,
     wg, res,
-    v, vt, wide, narrow, pf, yv, u, k, kf, kw, cot, onehot, rg, gains, st,
+    v, vt, wide, narrow, pf, yv, uk, k, kw, cot, onehot, rg, gains, st,
     qa0, qa1, qb0, qb1, ra0, ra1, rb0, rb1, ra20, ra21, rb20, rb21,
     local_sem,
     v_send, v_recv, v_other, k_send, k_recv, k_other, p_send, p_recv, p_end, s_send, s_recv,
@@ -103,7 +104,7 @@
 
     barrier = pltpu.get_barrier_semaphore()
     friends = [(lax.rem(g + n, GROUPS), d) for n in range(1, GROUPS)]
-    friends += [y_dev(1), y_dev(-1), z_dev(1), z_dev(-1)]
+    friends += [y_dev(n) for n in (1, 2, 3)] + [z_dev(n) for n in (1, 2, 3)]
     for friend in friends:
         pl.semaphore_signal(barrier, inc=1, device_id=friend, device_id_type=MESH)
     pl.semaphore_wait(barrier, len(friends))
@@ -209,6 +210,8 @@
     for n in range(CHUNKS):
         loads[4 + n].wait()
         p_own(n)
+    for n in range(CHUNKS):
+        p_spread(n, 0)
 
     tiles = []
     earlier = [jnp.int32(0)] * GROUPS
@@ -258,25 +261,32 @@
                 both = [bufs[n, 2 * i].astype(F32), bufs[n, 2 * i + 1].astype(F32)]
                 pf[part, n * width : (n + 1) * width] = jnp.concatenate(both, axis=0).astype(BF16)
 
-    def project(pair, i):
+    def project(pair, row, count):
         first, last = ((0, 2 * WIDE), (2 * WIDE, WIDTH))[pair]
-        part = slice(i * 512, (i + 1) * 512)
+        part = pl.ds(pl.multiple_of(row, 2 * ROWS), count)
         yv[part, first:last] = jnp.dot(
             v[part, :], pf[:, : last - first], preferred_element_type=F32
         ).astype(BF16)
 
+    def project_chip(by):
+        project(0, step(x, by) * 2 * ROWS, 2 * ROWS)
+
+    def key_side(slot):
+        part = pl.ds(slot * CAP, CAP)
+        product = lax.dot_general(
+            k[part].reshape(SLOT_ROWS, KEYS), kw[...], (((1,), (1,)), ((), ())),
+            preferred_element_type=F32,
+        )
+        uk[part] = (gains[...].astype(F32).reshape(1, WIDTH) * product).reshape(CAP, TROWS, WIDTH)
+
     for n in (0, 1):
         p_first(n)
-    for n in (0, 1):
-        p_spread(n, 0)
     for i in range(ROW_PIECES):
         rows.own_other(i)
     for n in (2, 3):
         p_first(n)
     for n in (0, 1):
         p_first_spread(n)
-    for n in (2, 3):
-        p_spread(n, 0)
     rows.near(0)
     for n in (2, 3):
         p_first_spread(n)
@@ -293,6 +303,9 @@
     for n in (0, 1):
         p_second(n, 1)
     rows.near(3)
+    loads[2].wait()
+    loads[8].wait()
+    key_side(g)
     for n in (0, 1):
         p_second(n, 2)
     transpose(x_slot(-s, c))
@@ -304,57 +317,65 @@
     rows.from_other(1)
     transpose(x_slot(s, 1 - c))
     rows.far(2)
+    for n in (2, 3):
+        p_second(n, 0)
     rows.from_other(2)
     transpose(x_slot(-s, 1 - c))
     rows.far(3)
     for n in (2, 3):
-        for j in (0, 1):
-            p_second(n, j)
-    transpose(x_slot(2, c))
+        p_second(n, 1)
+    keys.from_other(0)
+    key_side(x_slot(0, 1 - c))
+    for n in (2, 3):
+        p_second(n, 2)
     for n in (0, 1):
         p_last(n)
     assemble(0)
+    keys.near(0)
+    project_chip(0)
     for n in (2, 3):
-        for j in (2, 3):
-            p_second(n, j)
-    keys.near(0)
+        p_second(n, 3)
+    keys.near(1)
+    project_chip(-s)
+    project_chip(s)
+    keys.from_other(1)
+    key_side(x_slot(s, 1 - c))
     rows.from_other(3)
-    project(0, 0)
-    keys.near(1)
-    project(0, 1)
     keys.far(0)
+    project_chip(2)
+    key_side(x_slot(-s, c))
+    key_side(x_slot(s, c))
+    keys.from_other(2)
+    key_side(x_slot(-s, 1 - c))
+    keys.far(1)
     for n in (2, 3):
         p_last(n)
     assemble(1)
-    project(1, 0)
-    keys.far(1)
-    project(1, 1)
-    for m in range(4):
-        keys.from_other(m)
-    for i, (target, slot, _) in enumerate(tiles):
-        kf[i * TROWS : (i + 1) * TROWS, :] = k[target * CAP + slot]
-    loads[2].wait()
-    loads[8].wait()
-    gain_row = gains[...].astype(F32).reshape(1, WIDTH)
-    for i in range(2):
-        part = slice(i * 512, (i + 1) * 512)
-        u[part, :] = gain_row * lax.dot_general(
-            kf[part, :], kw[...], (((1,), (1,)), ((), ())), preferred_element_type=F32
-        )
+    project(1, 0, 512)
+    project(1, 512, 512)
+    key_side(x_slot(2, c))
+    keys.from_other(3)
+    key_side(x_slot(2, 1 - c))
 
     for i in range(GROUPS):
-        part = slice(i * ROWS, (i + 1) * ROWS)
-        squares = jnp.zeros((ROWS, 128), F32)
-        products = jnp.zeros((ROWS, 128), F32)
-        for j in range(WIDTH // 128):
-            cols = slice(j * 128, (j + 1) * 128)
-            value = yv[part, cols].astype(F32)
-            squares += value * value
-            products += value * u[part, cols]
-        st[g, pl.ds(i, 1), :] = jnp.sum(squares.T, axis=0, keepdims=True)
-        st[g, pl.ds(GROUPS + i, 1), :] = jnp.sum(products.T, axis=0, keepdims=True)
+        sums = []
+        for n in range(i * TILES, (i + 1) * TILES):
+            target, slot, _ = tiles[n]
+            side = uk[target * CAP + slot]
+            squares = jnp.zeros((TROWS, 128), F32)
+            products = jnp.zeros((TROWS, 128), F32)
+            for j in range(WIDTH // 128):
+                cols = slice(j * 128, (j + 1) * 128)
+                value = yv[n * TROWS : (n + 1) * TROWS, cols].astype(F32)
+                squares += value * value
+                products += value * side[:, cols]
+            sums.append((squares, products))
+        for m in range(2):
+            block = jnp.concatenate([pair[m] for pair in sums], axis=0)
+            st[g, pl.ds(m * GROUPS + i, 1), :] = jnp.sum(block.T, axis=0, keepdims=True)
     for n in range(1, GROUPS):
         start(st.at[g], st.at[g], s_send.at[0], s_recv.at[0], (lax.rem(g + n, GROUPS), d))
+    transpose(x_slot(2, c))
     transpose(x_slot(2, 1 - c))
     done(st.at[pl.ds(0, GROUPS - 1)], s_recv.at[0])
     total = st[0]
@@ -364,13 +385,17 @@
     inverse = lax.rsqrt(mean[:GROUPS] + norm_eps)
     inner = inverse * mean[GROUPS:]
     for i in range(GROUPS):
-        part = slice(i * ROWS, (i + 1) * ROWS)
         inv = jnp.broadcast_to(inverse[i : i + 1], (ROWS, 128)).T
         inn = jnp.broadcast_to((inverse * inner)[i : i + 1], (ROWS, 128)).T
-        for j in range(WIDTH // 128):
-            cols = slice(j * 128, (j + 1) * 128)
-            value = yv[part, cols].astype(F32)
-            rg[part, cols] = (inv * (u[part, cols] - value * inn)).astype(BF16)
+        for n in range(TILES):
+            target, slot, _ = tiles[i * TILES + n]
+            side = uk[target * CAP + slot]
+            here = slice(n * TROWS, (n + 1) * TROWS)
+            rows_here = slice((i * TILES + n) * TROWS, (i * TILES + n + 1) * TROWS)
+            for j in range(WIDTH // 128):
+                cols = slice(j * 128, (j + 1) * 128)
+                value = yv[rows_here, cols].astype(F32)
+                rg[rows_here, cols] = (inv[here] * (side[:, cols] - value * inn[here])).astype(BF16)
 
     loads[3].wait()
     lead_y = 1 - lax.div(y, 2)
@@ -403,6 +428,12 @@
         def long(self, i):
             self.send(0, i, 2, s)
 
+        def long_block(self, i, j):
+            start(
+                self.q.at[self.piece(2, i), j], self.r.at[4 + i, j],
+                q_send.at[self.n], q_long.at[self.n, i], self.near(s),
+            )
+
         def plain(self, i):
             self.send(1, i, -s, -s)
 
@@ -444,6 +475,20 @@
             here = self.block(s)
             self.q[here] = (self.q[here].astype(F32) + self.r2[2].astype(F32)).astype(BF16)
             self.send2(2, s, s)
+
+        def direct2(self):
+            for m in range(1, RING):
+                start(
+                    self.q.at[self.block(m)], self.r2.at[m - 1],
+                    q2_send.at[self.n], q2_near.at[self.n], self.near2(m),
+                )
+
+        def finish_direct(self, cols):
+            done(self.r2, q2_near.at[self.n])
+            total = self.q[self.block(0)].astype(F32)
+            for m in range(RING - 1):
+                total = total + self.r2[m].astype(F32)
+            wg[:, cols] = total
 
         def finish(self, cols):
             done(self.r2.at[pl.ds(0, 2)], q2_near.at[self.n])
@@ -465,9 +510,10 @@
             )
         )
 
-    for (a, b), (first, width) in zip(sums, PARTS):
-
-        @pl.loop(0, 8)
+    def turns(n, begin, end):
+        (a, b), (first, width) = sums[n], PARTS[n]
+
+        @pl.loop(begin, end)
         def _(i):
             turn, which = lax.div(i, 2), lax.rem(i, 2)
             by = jnp.where(turn == 0, 2, jnp.where(turn == 1, -s, jnp.where(turn == 2, s, 0)))
@@ -484,27 +530,40 @@
             b.q[4 * pair + lax.div(plane, 2), lax.rem(plane, 2)] = low
             b.q[4 * pair + 2 + lax.div(plane, 2), lax.rem(plane, 2)] = high
             for n in range(2):
-                pl.when(i == 1 + 2 * n)(lambda n=n: b.long(n))
                 pl.when(i == 5 + 2 * n)(lambda n=n: b.plain(n))
-
-    for pair in sums:
-        for i in range(2):
-            for part in pair:
-                part.middle(i)
-    for pair in sums:
-        for i in range(2):
-            for part in pair:
-                part.own(i)
-                if i == 0:
-                    part.long2()
-        for part in pair:
-            part.plain2()
-    for pair in sums:
-        for part in pair:
-            part.middle2()
-    for (a, b), (first, width) in zip(sums, PARTS):
-        a.finish(slice(first, first + width))
-        b.finish(slice(HALF + first, HALF + first + width))
+            for n in range(4):
+                pl.when(i == n)(lambda n=n: b.long_block(n // 2, n % 2))
+
+    def middles(n, i):
+        for part in sums[n]:
+            part.middle(i)
+
+    turns(0, 0, 8)
+    turns(1, 0, 4)
+    middles(0, 0)
+    turns(1, 4, 8)
+    middles(0, 1)
+    middles(1, 0)
+    middles(1, 1)
+    early, late = sums
+    for i in range(2):
+        for part in early:
+            part.own(i)
+            if i == 0:
+                part.long2()
+    for part in early:
+        part.plain2()
+    for part in early:
+        part.middle2()
+    for i in range(2):
+        for part in late:
+            part.own(i)
+    for part in late:
+        part.direct2()
+    for pair, (first, width) in zip(sums, PARTS):
+        for n, part in enumerate(pair):
+            cols = slice(n * HALF + first, n * HALF + first + width)
+            part.finish(cols) if pair is early else part.finish_direct(cols)
 
     done(v.at[pl.ds(0, 7 * ROWS)], v_send.at[0])
     done(k.at[pl.ds(0, 7 * CAP)], k_send.at[0])
@@ -516,11 +575,23 @@
             part.sent()
 
 
+def write_back(grad, left, grad_out, left_out, sems):
+    copies = []
+    for i in range(WRITES):
+        part = pl.ds(i * (ENC // WRITES), ENC // WRITES)
+        copies.append(pltpu.make_async_copy(left.at[part], left_out.at[part], sems.at[i]))
+    copies.append(pltpu.make_async_copy(grad, grad_out, sems.at[WRITES]))
+    for copy in copies:
+        copy.start()
+    for copy in copies:
+        copy.wait()
+
+
 def per_device(visual, projector, key_weight, norm_gain, cotangent, residual, counts, offsets):
     anywhere = pl.BlockSpec(memory_space=pl.ANY)
     scalars = pl.BlockSpec(memory_space=pltpu.SMEM)
     dma = pltpu.SemaphoreType.DMA
-    return pl.pallas_call(
+    results = pl.pallas_call(
         kernel,
         out_shape=(
             pltpu.VMEM((BLOCK, WIDTH), F32),
@@ -537,9 +608,8 @@
             pltpu.VMEM((2, 16, BLOCK, NARROW), BF16),
             pltpu.VMEM((ENC, 2 * WIDE), BF16),
             pltpu.VMEM((ALL_ROWS, WIDTH), BF16),
-            pltpu.VMEM((ALL_ROWS, WIDTH), F32),
+            pltpu.VMEM((GROUPS * CAP, TROWS, WIDTH), F32),
             pltpu.VMEM((GROUPS * CAP, TROWS, KEYS), BF16),
-            pltpu.VMEM((ALL_ROWS, KEYS), BF16),
             pltpu.VMEM((WIDTH, KEYS), BF16),
             pltpu.VMEM((512, KEYS), BF16),
             pltpu.VMEM((SLOT_ROWS, 512), BF16),
@@ -559,12 +629,24 @@
             dma((4,)), dma((4, 2)), dma((4, 2)), dma((4,)), dma((4,)), dma((4,)),
         ],
         compiler_params=pltpu.CompilerParams(
-            collective_id=0, has_side_effects=True, vmem_limit_bytes=54 * 2**20
+            collective_id=0, has_side_effects=True, vmem_limit_bytes=56 * 2**20
         ),
         cost_estimate=pl.CostEstimate(flops=16 * 10**9, bytes_accessed=20 * 10**6, transcendentals=0),
     )(
         visual[0], projector, key_weight, norm_gain, cotangent[0], residual, counts[0], offsets[0]
     )
+    grad, left = [pltpu.with_memory_space_constraint(r, pltpu.VMEM) for r in results]
+    return pl.pallas_call(
+        write_back,
+        out_shape=(
+            jax.ShapeDtypeStruct((BLOCK, WIDTH), F32),
+            jax.ShapeDtypeStruct((ENC, WIDTH), BF16),
+        ),
+        in_specs=[pl.BlockSpec(memory_space=pltpu.VMEM)] * 2,
+        out_specs=(anywhere, anywhere),
+        scratch_shapes=[dma((WRITES + 1,))],
+        compiler_params=pltpu.CompilerParams(vmem_limit_bytes=2**20),
+    )(grad, left)
 
 
 def solution(mesh):

time: 106 us -> 105 us (level)
  local copies, waits for them, and re-layouts: 3.68 us -> 0 us
  Pallas kernels: 102 us -> 104 us
    unnamed x2 -> x0, local copies, waits for them, and re-layouts: 3.68 us -> none
    pallas_call x0 -> x1, Pallas kernels: none -> 3.08 us  [per_device(): pl.pallas_call(write_back, out_shape=(jax.ShapeDtypeStruct((BLOCK, WIDTH)...]
    pallas_call x1, Pallas kernels: 102 us -> 101 us  [per_device(): pl.pallas_call(kernel, out_shape=(pltpu.VMEM((BLOCK, WIDTH), F32), pltpu....]
where the time goes in v3:
time: 105 us; the launch traced here: 104 us
  Pallas kernels  104 us (99%)
    pallas_call x1, Pallas kernels, per_device(): pl.pallas_call(kernel, out_shape=(pltpu.VMEM((BLOCK, WIDTH), F32), pltpu....  101 us
    pallas_call x1, Pallas kernels, per_device(): pl.pallas_call(write_back, out_shape=(jax.ShapeDtypeStruct((BLOCK, WIDTH)...  3.08 us

profile of v3, /device:TPU:0, one launch (start us, length us, event | category | flops | bytes accessed | tf_op | source)
XLA Modules:
  0.0 104.5 jit_solution(16803357106244916293)
XLA Ops:
  0.6 100.8 %shard_map.95 = (f32[200,1024]{1,0:T(8,128)S(1)}, bf16[3200,1024]{1,0:T(8,128)(2,1)S(1)}) custom-call(bf16[128,3200]{1,0:T(8,128)(2,1)} %bitcast.4, bf16[200,1024]{1,0:T(8,128)(2,1)} %projector.1, bf16[8192,512]{1,0:T(8,128)(2,1)} %key_weight.1, bf16[8192]{0:T(1024)(128)(2,1)} %gain.1, bf16[512,512]{1,0:T(8,128)(2,1)} %bitcast.5, ...), custom_call_target="tpu_custom_call" | custom-call | flops 16000000000 | bytes 20000000 | tf_op jit(solution)/shard_map/pallas_call | solution.py:594
  101.4 3.1 %shard_map.96 = (f32[200,1024]{1,0:T(8,128)}, bf16[3200,1024]{1,0:T(8,128)(2,1)}) custom-call(f32[200,1024]{1,0:T(8,128)S(1)} %get-tuple-element.4.grad, bf16[3200,1024]{1,0:T(8,128)(2,1)S(1)} %get-tuple-element.5.left), custom_call_target="tpu_custom_call" | custom-call | tf_op jit(solution)/shard_map/pallas_call | solution.py:639

commit v4 on v3

--- a/solution.py
+++ b/solution.py
@@ -553,13 +553,13 @@
                 part.long2()
     for part in early:
         part.plain2()
-    for part in early:
-        part.middle2()
     for i in range(2):
         for part in late:
             part.own(i)
     for part in late:
         part.direct2()
+    for part in early:
+        part.middle2()
     for pair, (first, width) in zip(sums, PARTS):
         for n, part in enumerate(pair):
             cols = slice(n * HALF + first, n * HALF + first + width)

time: 105 us -> 104 us (level)
  no operation moved by 1% of the time
where the time goes in v4:
time: 104 us
  Pallas kernels  103 us (99%)
    pallas_call x1, Pallas kernels, per_device(): pl.pallas_call(kernel, out_shape=(pltpu.VMEM((BLOCK, WIDTH), F32), pltpu....  99.8 us
    pallas_call x1, Pallas kernels, per_device(): pl.pallas_call(write_back, out_shape=(jax.ShapeDtypeStruct((BLOCK, WIDTH)...  3.08 us

profile of v4, /device:TPU:0, one launch (start us, length us, event | category | flops | bytes accessed | tf_op | source)
XLA Modules:
  0.0 103.5 jit_solution(8945113856023211110)
XLA Ops:
  0.6 99.8 %shard_map.95 = (f32[200,1024]{1,0:T(8,128)S(1)}, bf16[3200,1024]{1,0:T(8,128)(2,1)S(1)}) custom-call(bf16[128,3200]{1,0:T(8,128)(2,1)} %bitcast.4, bf16[200,1024]{1,0:T(8,128)(2,1)} %projector.1, bf16[8192,512]{1,0:T(8,128)(2,1)} %key_weight.1, bf16[8192]{0:T(1024)(128)(2,1)} %gain.1, bf16[512,512]{1,0:T(8,128)(2,1)} %bitcast.5, ...), custom_call_target="tpu_custom_call" | custom-call | flops 16000000000 | bytes 20000000 | tf_op jit(solution)/shard_map/pallas_call | solution.py:594
  100.4 3.1 %shard_map.96 = (f32[200,1024]{1,0:T(8,128)}, bf16[3200,1024]{1,0:T(8,128)(2,1)}) custom-call(f32[200,1024]{1,0:T(8,128)S(1)} %get-tuple-element.4.grad, bf16[3200,1024]{1,0:T(8,128)(2,1)S(1)} %get-tuple-element.5.left), custom_call_target="tpu_custom_call" | custom-call | tf_op jit(solution)/shard_map/pallas_call | solution.py:639
